TPU v7x, 32 devices: a whole 2x2x4 slice. The times are simulated.
32 devices in a mesh: dp: 4 (over y, core), mp: 8 (over z, x).
Axes of the slice: x: 2, y: 2, z: 4, core: 2. Of those that a mesh axis runs over, the one named last changes fastest.
Arguments:
- tokens: bfloat16 [32768, 1024], P(('dp', 'mp')), may hold values from -6 to 6
- segment_ids: int32 [32, 1024], P(('dp', 'mp')), may hold values from 0 to 15, never falling along the last dimension, each value on 1 to 256 neighbouring positions
- w_query: bfloat16 [1024, 1024], replicated, may hold values from -0.1875 to 0.1875
- w_key: bfloat16 [1024, 1024], replicated, may hold values from -0.1875 to 0.1875
- w_value: bfloat16 [1024, 1024], replicated, may hold values from -0.1875 to 0.1875
- w_out: bfloat16 [1024, 1024], replicated, may hold values from -2 to 2
- gain_one: float32 [1024], replicated, may hold values from 0.5 to 1.5
- gain_two: float32 [1024], replicated, may hold values from 0.5 to 1.5
- w_in: bfloat16 [1024, 4096], P(None, 'mp'), may hold values from -0.1875 to 0.1875
- w_back: bfloat16 [4096, 1024], P('mp'), may hold values from -0.09375 to 0.09375
- prefix_master: float32 [2, 64, 1024], replicated, may hold values from -6 to 6
- moment_one: float32 [2, 64, 1024], replicated, may hold values from -6 to 6
- moment_two: float32 [2, 64, 1024], replicated, may hold values from 0.064 to 1.024
- cotangent: bfloat16 [32768, 1024], P(('dp', 'mp')), may hold values from -6 to 6
Outputs:
- layer_output: bfloat16 [32768, 1024], P(('dp', 'mp'))
- input_grad: float32 [32768, 1024], P(('dp', 'mp'))
- new_master: float32 [2, 64, 1024], replicated
- new_first: float32 [2, 64, 1024], replicated
- new_second: float32 [2, 64, 1024], replicated
- new_copy: bfloat16 [2, 64, 1024], replicated
Inputs may be any that keep to these rules, and one draw needn't show every extreme that they name: `segment_ids`: within each packed row the ids never fall, start at 0 and number whole sentences of 1 to 256 tokens, one of exactly that length.
All inputs are finite; a program needn't handle non-finite values.
Results may differ from a plain program's by a relative error of at most 0.014.
Values may be sent and summed in bfloat16 or wider, within the bound.
No kernel may reach another device: no remote copies, remote signals or barrier semaphores. Data moves between devices by JAX's collectives and lax.ppermute only.
A program may use at most 320 MiB of HBM per device.

v0:
```python
import jax
import jax.numpy as jnp
from jax import lax
from jax.sharding import PartitionSpec as P

HEADS = 16
STEP = 5


epsilon_norm = 1e-05
masked_score = -1e30
learn_rate = 1.0
weight_decay = 0.01
beta_one = 0.9
beta_two = 0.999
epsilon_adam = 1e-08


def layer_norm(values, gain):
    average = jnp.mean(values, axis=-1, keepdims=True)
    centred = values - average
    spread = jnp.mean(centred * centred, axis=-1, keepdims=True)
    return gain * centred * lax.rsqrt(spread + epsilon_norm)


def gelu_exact(values):
    return jax.nn.gelu(values, approximate=False)


def dot_right(left, right):
    return lax.dot_general(
        left, right, (((1,), (1,)), ((), ())), preferred_element_type=jnp.float32
    )


def block_scores(q_block, seg_block, keys_row, seg_row, prefix_keys, score_scale):
    pre_score = (
        jnp.einsum("bhd,phd->hbp", q_block, prefix_keys, preferred_element_type=jnp.float32)
        * score_scale
    )
    own_score = (
        jnp.einsum("bhd,khd->hbk", q_block, keys_row, preferred_element_type=jnp.float32)
        * score_scale
    )
    same_segment = (seg_block[:, None] == seg_row[None, :])[None]
    own_score = jnp.where(same_segment, own_score, masked_score)
    return (pre_score, own_score)


def attend_row(
    queries, keys_row, values_row, seg_row, prefix_keys, prefix_vals, block_rows, score_scale
):
    length, head_count, head_width = queries.shape
    block_count = length // block_rows
    q_blocks = queries.reshape(block_count, block_rows, head_count, head_width)
    s_blocks = seg_row.reshape(block_count, block_rows)

    def one_block(pieces):
        q_block, seg_block = pieces
        pre_score, own_score = block_scores(
            q_block, seg_block, keys_row, seg_row, prefix_keys, score_scale
        )
        row_top = jnp.maximum(jnp.max(pre_score, axis=-1), jnp.max(own_score, axis=-1))[..., None]
        pre_exp = jnp.exp(pre_score - row_top)
        own_exp = jnp.exp(own_score - row_top)
        denominator = jnp.sum(pre_exp, axis=-1, keepdims=True) + jnp.sum(
            own_exp, axis=-1, keepdims=True
        )
        pre_weight = (pre_exp / denominator).astype(jnp.bfloat16)
        own_weight = (own_exp / denominator).astype(jnp.bfloat16)
        attended = jnp.einsum(
            "hbp,phd->bhd", pre_weight, prefix_vals, preferred_element_type=jnp.float32
        )
        attended = attended + jnp.einsum(
            "hbk,khd->bhd", own_weight, values_row, preferred_element_type=jnp.float32
        )
        return (attended, row_top + jnp.log(denominator))

    attended, log_sum = lax.map(one_block, (q_blocks, s_blocks))
    return (attended.reshape(length, head_count, head_width), log_sum)


def attend_row_back(
    queries,
    keys_row,
    values_row,
    seg_row,
    prefix_keys,
    prefix_vals,
    log_sum,
    grad_att,
    block_rows,
    score_scale,
):
    length, head_count, head_width = queries.shape
    block_count = length // block_rows
    q_blocks = queries.reshape(block_count, block_rows, head_count, head_width)
    s_blocks = seg_row.reshape(block_count, block_rows)
    g_blocks = grad_att.reshape(block_count, block_rows, head_count, head_width)
    prefix_count = prefix_keys.shape[0]

    def one_block(carry, pieces):
        key_acc, val_acc, pk_acc, pv_acc = carry
        q_block, seg_block, g_block, l_block = pieces
        pre_score, own_score = block_scores(
            q_block, seg_block, keys_row, seg_row, prefix_keys, score_scale
        )
        pre_prob = jnp.exp(pre_score - l_block)
        own_prob = jnp.exp(own_score - l_block)
        pre_dot = jnp.einsum(
            "bhd,phd->hbp", g_block, prefix_vals, preferred_element_type=jnp.float32
        )
        own_dot = jnp.einsum(
            "bhd,khd->hbk", g_block, values_row, preferred_element_type=jnp.float32
        )
        center = jnp.sum(pre_prob * pre_dot, axis=-1, keepdims=True) + jnp.sum(
            own_prob * own_dot, axis=-1, keepdims=True
        )
        pre_ds = (pre_prob * (pre_dot - center)).astype(jnp.bfloat16)
        own_ds = (own_prob * (own_dot - center)).astype(jnp.bfloat16)
        q_grad = jnp.einsum("hbp,phd->bhd", pre_ds, prefix_keys, preferred_element_type=jnp.float32)
        q_grad = (
            q_grad
            + jnp.einsum("hbk,khd->bhd", own_ds, keys_row, preferred_element_type=jnp.float32)
        ) * score_scale
        key_acc = (
            key_acc
            + jnp.einsum("hbk,bhd->khd", own_ds, q_block, preferred_element_type=jnp.float32)
            * score_scale
        )
        pk_acc = (
            pk_acc
            + jnp.einsum("hbp,bhd->phd", pre_ds, q_block, preferred_element_type=jnp.float32)
            * score_scale
        )
        val_acc = val_acc + jnp.einsum(
            "hbk,bhd->khd",
            own_prob.astype(jnp.bfloat16),
            g_block,
            preferred_element_type=jnp.float32,
        )
        pv_acc = pv_acc + jnp.einsum(
            "hbp,bhd->phd",
            pre_prob.astype(jnp.bfloat16),
            g_block,
            preferred_element_type=jnp.float32,
        )
        return ((key_acc, val_acc, pk_acc, pv_acc), q_grad)

    row_zeros = jnp.zeros((length, head_count, head_width), jnp.float32)
    pre_zeros = jnp.zeros((prefix_count, head_count, head_width), jnp.float32)
    sums, q_grads = lax.scan(
        one_block,
        (row_zeros, row_zeros, pre_zeros, pre_zeros),
        (q_blocks, s_blocks, g_blocks, log_sum),
    )
    return (q_grads.reshape(length, head_count, head_width), sums[0], sums[1], sums[2], sums[3])


def on_device(
    tokens,
    segment_ids,
    w_query,
    w_key,
    w_value,
    w_out,
    gain_one,
    gain_two,
    w_in,
    w_back,
    prefix_master,
    moment_one,
    moment_two,
    cotangent,
):
    tok_count, model_width = tokens.shape
    row_count, length = segment_ids.shape
    head_count = HEADS
    head_width = model_width // head_count
    score_scale = head_width ** (-0.5)
    block_rows = min(512, length)

    def by_heads(values):
        return values.reshape(row_count, length, head_count, head_width)

    queries = jnp.dot(tokens, w_query, preferred_element_type=jnp.float32).astype(jnp.bfloat16)
    keys_own = jnp.dot(tokens, w_key, preferred_element_type=jnp.float32).astype(jnp.bfloat16)
    values_own = jnp.dot(tokens, w_value, preferred_element_type=jnp.float32).astype(jnp.bfloat16)
    prefix_low = prefix_master.astype(jnp.bfloat16)
    prefix_keys = prefix_low[0].reshape(-1, head_count, head_width)
    prefix_vals = prefix_low[1].reshape(-1, head_count, head_width)

    def forward_row(pieces):
        q_row, k_row, v_row, s_row = pieces
        return attend_row(
            q_row, k_row, v_row, s_row, prefix_keys, prefix_vals, block_rows, score_scale
        )

    attended, log_sum = lax.map(
        forward_row, (by_heads(queries), by_heads(keys_own), by_heads(values_own), segment_ids)
    )
    attended_low = attended.reshape(tok_count, model_width).astype(jnp.bfloat16)
    sum_one = tokens.astype(jnp.float32) + jnp.dot(
        attended_low, w_out, preferred_element_type=jnp.float32
    )
    normed_one = layer_norm(sum_one, gain_one)
    normed_low = normed_one.astype(jnp.bfloat16)
    pre_act = jnp.dot(
        lax.all_gather(normed_low, "mp", axis=0, tiled=True),
        w_in,
        preferred_element_type=jnp.float32,
    )
    activation = gelu_exact(pre_act).astype(jnp.bfloat16)
    branch = lax.psum_scatter(
        jnp.dot(activation, w_back, preferred_element_type=jnp.float32).astype(jnp.bfloat16),
        "mp",
        scatter_dimension=0,
        tiled=True,
    ).astype(jnp.float32)
    sum_two = normed_one + branch
    layer_output = layer_norm(sum_two, gain_two).astype(jnp.bfloat16)

    def norm_two(values):
        return layer_norm(values, gain_two)

    def norm_one(values):
        return layer_norm(values, gain_one)

    grad_two = jax.vjp(norm_two, sum_two)[1](cotangent.astype(jnp.float32))[0]
    grad_low = grad_two.astype(jnp.bfloat16)
    grad_act = dot_right(lax.all_gather(grad_low, "mp", axis=0, tiled=True), w_back)
    grad_pre = jax.vjp(gelu_exact, pre_act)[1](grad_act)[0].astype(jnp.bfloat16)
    grad_ffn = lax.psum_scatter(
        dot_right(grad_pre, w_in).astype(jnp.bfloat16), "mp", scatter_dimension=0, tiled=True
    ).astype(jnp.float32)
    grad_normed = grad_two + grad_ffn
    grad_one = jax.vjp(norm_one, sum_one)[1](grad_normed)[0]
    grad_att = dot_right(grad_one.astype(jnp.bfloat16), w_out).astype(jnp.bfloat16)

    def backward_row(pieces):
        q_row, k_row, v_row, s_row, l_row, g_row = pieces
        return attend_row_back(
            q_row,
            k_row,
            v_row,
            s_row,
            prefix_keys,
            prefix_vals,
            l_row,
            g_row,
            block_rows,
            score_scale,
        )

    q_grads, k_grads, v_grads, pk_grads, pv_grads = lax.map(
        backward_row,
        (
            by_heads(queries),
            by_heads(keys_own),
            by_heads(values_own),
            segment_ids,
            log_sum,
            by_heads(grad_att),
        ),
    )
    grad_query = q_grads.reshape(tok_count, model_width).astype(jnp.bfloat16)
    grad_key = k_grads.reshape(tok_count, model_width).astype(jnp.bfloat16)
    grad_value = v_grads.reshape(tok_count, model_width).astype(jnp.bfloat16)
    input_grad = (
        grad_one
        + dot_right(grad_query, w_query)
        + dot_right(grad_key, w_key)
        + dot_right(grad_value, w_value)
    )
    local_prefix = jnp.stack(
        [
            jnp.sum(pk_grads, axis=0).reshape(-1, model_width),
            jnp.sum(pv_grads, axis=0).reshape(-1, model_width),
        ]
    )
    prefix_grad = lax.psum(local_prefix, ("dp", "mp"))
    new_first = beta_one * moment_one + (1.0 - beta_one) * prefix_grad
    new_second = beta_two * moment_two + (1.0 - beta_two) * prefix_grad * prefix_grad
    first_hat = new_first / (1.0 - beta_one**STEP)
    second_hat = new_second / (1.0 - beta_two**STEP)
    new_master = prefix_master * (1.0 - learn_rate * weight_decay) - learn_rate * first_hat / (
        jnp.sqrt(second_hat) + epsilon_adam
    )
    return (
        layer_output,
        input_grad,
        new_master,
        new_first,
        new_second,
        new_master.astype(jnp.bfloat16),
    )


def solution(mesh):
    return jax.shard_map(
        on_device,
        mesh=mesh,
        in_specs=(
            P(("dp", "mp"), None),
            P(("dp", "mp"), None),
            P(),
            P(),
            P(),
            P(),
            P(),
            P(),
            P(None, "mp"),
            P("mp", None),
            P(),
            P(),
            P(),
            P(("dp", "mp"), None),
        ),
        out_specs=(P(("dp", "mp"), None), P(("dp", "mp"), None), P(), P(), P(), P()),
        check_vma=False,
    )
```

profile of v0, /device:TPU:0, one launch (start us, length us, event | category | flops | bytes accessed | tf_op | source)
XLA Modules:
  0.0 1698.9 jit_solution(10154313430117699691)
XLA Ops:
  43.6 101.2 %while.55 = (s32[]{:T(128)}, bf16[2,512,16,64]{1,3,2,0:T(8,128)(2,1)}, f32[2,16,512,1]{2,1,3,0:T(8,128)S(1)}, bf16[2,512,16,64]{1,3,2,0:T(8,128)(2,1)}, bf16[64,...) while((s32[]{:T(128)}, ...), condition=%wide.region_5.6_spmd, body=%wide.region_0.5_spmd.sunk | while | flops 2388123648 | bytes 156314352 | solution.py:79
  44.2 15.8 fusion.157
  60.4 15.1 fusion.159
  76.0 16.1 fusion.160
  94.6 15.8 fusion.157
  110.8 15.1 fusion.159
  126.3 16.1 fusion.160
  156.5 230.4 %all-gather.3.cloned.1.call-done = bf16[8192,1024]{0,1:T(8,128)(2,1)} async-done(((bf16[1024,1024]{0,1:T(8,128)(2,1)}), bf16[8192,1024]{0,1:T(8,128)(2,1)}) %all-gather.3.cloned.1.call-update) | async-done | bytes 16777232 | tf_op jit(solution)/shard_map/all_gather | solution.py:209
  386.9 46.5 %fusion.56 = (f32[8192,512]{1,0:T(8,128)}, f32[8192,512]{1,0:T(8,128)}) fusion(bf16[8192,1024]{0,1:T(8,128)(2,1)} %all-gather.3.cloned.1.call-done, bf16[1024,512]{1,0:T(8,128)(2,1)} %param.26), kind=kOutput, calls=%fused_computation.78 | convolution fusion | flops 8849981440 | bytes 51380224 | tf_op jit(solution)/shard_map/dot_general | solution.py:208
  433.4 21.3 %convolution_convert_fusion.1 = bf16[8192,1024]{0,1:T(8,128)(2,1)} fusion(bf16[512,1024]{1,0:T(8,128)(2,1)S(1)} %copy-done.40, f32[8192,512]{1,0:T(8,128)} %get-tuple-element.401, f32[8192,512]{1,0:T(8,128)} %get-tuple-element.402), kind=kOutput, calls=%fused_computation.95 | convolution fusion | flops 8610906112 | bytes 51380224 | tf_op jit(solution)/shard_map/dot_general | solution.py:215
  459.0 276.8 %reduce-scatter.3.cloned.1.call-done = bf16[1024,1024]{0,1:T(8,128)(2,1)} async-done(((bf16[8192,1024]{0,1:T(8,128)(2,1)}), bf16[1024,1024]{0,1:T(8,128)(2,1)}) %reduce-scatter.3.cloned.1.call-update) | async-done | bytes 2097168 | tf_op jit(solution)/shard_map/reduce_scatter | solution.py:214
  753.6 226.8 %all-gather.5.cloned.1.call-done = bf16[8192,1024]{0,1:T(8,128)(2,1)} async-done(((bf16[1024,1024]{0,1:T(8,128)(2,1)}), bf16[8192,1024]{0,1:T(8,128)(2,1)}) %all-gather.5.cloned.1.call-update) | async-done | bytes 16777232 | tf_op jit(solution)/shard_map/all_gather | solution.py:231
  980.4 32.0 %convolution_convert_fusion = bf16[8192,1024]{0,1:T(8,128)(2,1)} fusion(bf16[1024,512]{1,0:T(8,128)(2,1)} %param.26, f32[8192,512]{1,0:T(8,128)} %get-tuple-element.401, f32[8192,512]{1,0:T(8,128)} %get-tuple-element.402, bf16[8192,1024]{0,1:T(8,128)(2,1)} %all-gather.5.cloned.1.call-done, bf16[512,1024]{1,0:T(8,128)(2,1)S(1)} %copy-done.40), kind=kOutput, calls=%fused_computation.94 | convolution fusion | flops 17246978048 | bytes 69206016 | tf_op jit(solution)/shard_map/dot_general | solution.py:31
  1013.4 280.0 %reduce-scatter.5.cloned.1.call-done = bf16[1024,1024]{0,1:T(8,128)(2,1)} async-done(((bf16[8192,1024]{0,1:T(8,128)(2,1)}), bf16[1024,1024]{0,1:T(8,128)(2,1)}) %reduce-scatter.5.cloned.1.call-update) | async-done | bytes 2097168 | tf_op jit(solution)/shard_map/reduce_scatter | solution.py:233
  1325.0 233.9 %while.56 = (s32[]{:T(128)}, f32[1024,16,64]{0,2,1:T(8,128)}, f32[1024,16,64]{0,2,1:T(8,128)}, f32[64,16,64]{0,2,1:T(8,128)}, f32[64,16,64]{0,2,1:T(8,128)}, /*i...) while((s32[]{:T(128)}, f32[1024,16,64]{0,2,1:T(8,128)}, ...), condition=%wide.region_19.20_spmd.clone, body=%wide.region_16.19_spmd.clone.sunk | while | flops 5841412096 | bytes 375698496 | solution.py:152
  1325.2 14.6 fusion.179
  1340.2 25.8 %multiply_reduce_fusion.10 = (f32[16,512]{1,0:T(8,128)S(1)}, f32[16,512,1024]{2,1,0:T(8,128)}) fusion(f32[16,512,1024]{2,1,0:T(8,128)} %fusion.179, f32[16,512]{1,0:T(8,128)S(1)} %dynamic-slice_bitcast_fusion.2, pred[512,1024]{1,0:T(8,128)(4,1)S(1)} %broadcast_compare_fusion.5, bf16[1024,16,64]{0,2,1:T(8,128)(2,1)S(1)} %copy-done.16, ...), kind=kOutput, calls=%fused_computation.28.clone.1 | convolution fusion | flops 1115676672 | bytes 70844416 | tf_op jit(solution)/shard_map/while/body/eval_jaxpr/while/body/eval_jaxpr/bhd,khd->hbk/dot_general | solution.py:113
  1368.5 27.8 %multiply_convert_fusion.8 = bf16[16,512,1024]{2,1,0:T(8,128)(2,1)} fusion(f32[16,512,1024]{2,1,0:T(8,128)} %get-tuple-element.571, f32[16,512,1024]{2,1,0:T(8,128)} %fusion.179, f32[16,512]{1,0:T(8,128)S(1)} %add.232, f32[16,512]{1,0:T(8,128)S(1)} %dynamic-slice_bitcast_fusion.2, pred[512,1024]{1,0:T(8,128)(4,1)S(1)} %broadcast_compare_fusion.5), kind=kLoop, calls=%fused_computation.27.clone.1 | loop fusion | flops 50331648 | bytes 84475904 | tf_op jit(solution)/shard_map/while/body/eval_jaxpr/while/body/eval_jaxpr/convert_element_type | solution.py:120
  1419.8 17.7 %bitcast_add_fusion.5 = f32[1024,16,64]{0,2,1:T(8,128)} fusion(f32[1024,16,64]{0,2,1:T(8,128)} %get-tuple-element.627, f32[16,512,1024]{2,1,0:T(8,128)} %fusion.179, f32[16,512]{1,0:T(8,128)S(1)} %dynamic-slice_bitcast_fusion.2, pred[512,1024]{1,0:T(8,128)(4,1)} %copy-done.13, pred[]{:T(512)S(6)} %compare.3, ...), kind=kOutput, calls=%fused_computation.33.clone.1 | convolution fusion | flops 1109393408 | bytes 43549184 | tf_op jit(solution)/shard_map/while/body/eval_jaxpr/while/body/eval_jaxpr/hbk,bhd->khd/dot_general | solution.py:136
  1440.8 14.6 fusion.179
  1455.8 25.8 %multiply_reduce_fusion.10 = (f32[16,512]{1,0:T(8,128)S(1)}, f32[16,512,1024]{2,1,0:T(8,128)}) fusion(f32[16,512,1024]{2,1,0:T(8,128)} %fusion.179, f32[16,512]{1,0:T(8,128)S(1)} %dynamic-slice_bitcast_fusion.2, pred[512,1024]{1,0:T(8,128)(4,1)S(1)} %broadcast_compare_fusion.5, bf16[1024,16,64]{0,2,1:T(8,128)(2,1)S(1)} %copy-done.16, ...), kind=kOutput, calls=%fused_computation.28.clone.1 | convolution fusion | flops 1115676672 | bytes 70844416 | tf_op jit(solution)/shard_map/while/body/eval_jaxpr/while/body/eval_jaxpr/bhd,khd->hbk/dot_general | solution.py:113
  1484.1 27.8 %multiply_convert_fusion.8 = bf16[16,512,1024]{2,1,0:T(8,128)(2,1)} fusion(f32[16,512,1024]{2,1,0:T(8,128)} %get-tuple-element.571, f32[16,512,1024]{2,1,0:T(8,128)} %fusion.179, f32[16,512]{1,0:T(8,128)S(1)} %add.232, f32[16,512]{1,0:T(8,128)S(1)} %dynamic-slice_bitcast_fusion.2, pred[512,1024]{1,0:T(8,128)(4,1)S(1)} %broadcast_compare_fusion.5), kind=kLoop, calls=%fused_computation.27.clone.1 | loop fusion | flops 50331648 | bytes 84475904 | tf_op jit(solution)/shard_map/while/body/eval_jaxpr/while/body/eval_jaxpr/convert_element_type | solution.py:120
  1536.6 18.9 %bitcast_add_fusion.5 = f32[1024,16,64]{0,2,1:T(8,128)} fusion(f32[1024,16,64]{0,2,1:T(8,128)} %get-tuple-element.627, f32[16,512,1024]{2,1,0:T(8,128)} %fusion.179, f32[16,512]{1,0:T(8,128)S(1)} %dynamic-slice_bitcast_fusion.2, pred[512,1024]{1,0:T(8,128)(4,1)} %copy-done.13, pred[]{:T(512)S(6)} %compare.3, ...), kind=kOutput, calls=%fused_computation.33.clone.1 | convolution fusion | flops 1109393408 | bytes 43549184 | tf_op jit(solution)/shard_map/while/body/eval_jaxpr/while/body/eval_jaxpr/hbk,bhd->khd/dot_general | solution.py:136
  1589.7 99.7 %all-reduce.2.cloned.1.call-done = f32[2,64,1024]{2,1,0:T(8,128)} async-done(((f32[2,64,1024]{2,1,0:T(8,128)}), f32[2,64,1024]{2,1,0:T(8,128)}) %all-reduce.2.cloned.1.call-update) | async-done | bytes 524304 | tf_op jit(solution)/shard_map/psum | solution.py:281
  (268 shorter events, 202.8 us)
Async XLA Ops:
  7.2 142.2 %copy-start = (bf16[1024,1024]{1,0:T(8,128)(2,1)S(1)}, bf16[1024,1024]{1,0:T(8,128)(2,1)}, u32[]{:S(2)}) copy-start(bf16[1024,1024]{1,0:T(8,128)(2,1)} %param.23) | copy-start | bytes 6291460
  7.2 379.7 %all-gather.3.cloned.1.call-start = ((), (), s32[]{:S(2)}) async-start(), calls=%async_computation.2 | async-start | bytes 18874368 | tf_op jit(solution)/shard_map/all_gather | solution.py:209
  76.0 16.1 copy-start.29
  156.4 277.0 %copy-start.40 = (bf16[512,1024]{1,0:T(8,128)(2,1)S(1)}, bf16[512,1024]{1,0:T(8,128)(2,1)}, u32[]{:S(2)}) copy-start(bf16[512,1024]{1,0:T(8,128)(2,1)} %param.27) | copy-start | bytes 3145732
  156.5 579.3 %reduce-scatter.3.cloned.1.call-start = ((), (), s32[]{:S(2)}) async-start(), calls=%async_computation.3 | async-start | bytes 18874368 | tf_op jit(solution)/shard_map/reduce_scatter | solution.py:214
  454.8 281.0 %copy-start.47 = (f32[1024]{0:T(1024)S(1)}, f32[1024]{0:T(1024)}, u32[]{:S(2)}) copy-start(f32[1024]{0:T(1024)} %copy-done.46) | copy-start | bytes 12292
  454.8 281.0 %copy-start.49 = (f32[1024]{0:T(1024)S(1)}, f32[1024]{0:T(1024)}, u32[]{:S(2)}) copy-start(f32[1024]{0:T(1024)} %copy-done.48) | copy-start | bytes 12292
  454.8 281.0 %copy-start.51 = (f32[1024]{0:T(1024)S(1)}, f32[1024]{0:T(1024)}, u32[]{:S(2)}) copy-start(f32[1024]{0:T(1024)} %param.24) | copy-start | bytes 12292
  454.8 525.6 %all-gather.5.cloned.1.call-start = ((), (), s32[]{:S(2)}) async-start(), calls=%async_computation.4 | async-start | bytes 18874368 | tf_op jit(solution)/shard_map/all_gather | solution.py:231
  459.0 280.7 %copy-start.54 = (f32[1024]{0:T(1024)S(1)}, f32[1024]{0:T(1024)}, u32[]{:S(2)}) copy-start(f32[1024]{0:T(1024)} %param.25) | copy-start | bytes 12292
  753.6 539.9 %reduce-scatter.5.cloned.1.call-start = ((), (), s32[]{:S(2)}) async-start(), calls=%async_computation.5 | async-start | bytes 18874368 | tf_op jit(solution)/shard_map/reduce_scatter | solution.py:233
  1012.4 676.9 %all-reduce.2.cloned.1.call-start = ((), (), s32[]{:S(2)}) async-start(), calls=%async_computation.6 | async-start | bytes 1048576 | tf_op jit(solution)/shard_map/psum | solution.py:281
  1013.4 286.2 %copy-start.56 = (f32[1024]{0:T(1024)S(1)}, f32[1024]{0:T(1024)}, u32[]{:S(2)}) copy-start(f32[1024]{0:T(1024)} %copy-done.55) | copy-start | bytes 12292
  1325.2 40.8 %copy-start.27 = (bf16[64,16,64]{2,0,1:T(8,128)(2,1)}, bf16[64,16,64]{2,0,1:T(8,128)(2,1)S(1)}, u32[]{:S(2)}) copy-start(bf16[64,16,64]{2,0,1:T(8,128)(2,1)S(1)} %get-tuple-element.656) | copy-start | bytes 393220 | tf_op jit(solution)/shard_map/while/body/eval_jaxpr/while
  1340.2 28.4 %copy-start.13 = (pred[512,1024]{1,0:T(8,128)(4,1)}, pred[512,1024]{1,0:T(8,128)(4,1)S(1)}, u32[]{:S(2)}) copy-start(pred[512,1024]{1,0:T(8,128)(4,1)S(1)} %broadcast_compare_fusion.5) | copy-start | bytes 1572868 | tf_op jit(solution)/shard_map/while/body/eval_jaxpr/while
  1340.2 26.2 %copy-start.4 = (bf16[2,512,16,64]{1,3,2,0:T(8,128)(2,1)S(1)}, bf16[2,512,16,64]{1,3,2,0:T(8,128)(2,1)}, u32[]{:S(2)}) copy-start(bf16[2,512,16,64]{1,3,2,0:T(8,128)(2,1)} %get-tuple-element.648) | copy-start | bytes 6291460 | tf_op jit(solution)/shard_map/while/body/eval_jaxpr/while
  1419.8 17.7 %copy-start.23 = (f32[64,16,64]{0,2,1:T(8,128)S(1)}, f32[64,16,64]{0,2,1:T(8,128)}, u32[]{:S(2)}) copy-start(f32[64,16,64]{0,2,1:T(8,128)} %get-tuple-element.629) | copy-start | bytes 786436 | tf_op jit(solution)/shard_map/while/body/eval_jaxpr/while
  1440.8 40.8 %copy-start.27 = (bf16[64,16,64]{2,0,1:T(8,128)(2,1)}, bf16[64,16,64]{2,0,1:T(8,128)(2,1)S(1)}, u32[]{:S(2)}) copy-start(bf16[64,16,64]{2,0,1:T(8,128)(2,1)S(1)} %get-tuple-element.656) | copy-start | bytes 393220 | tf_op jit(solution)/shard_map/while/body/eval_jaxpr/while
  1455.7 28.4 %copy-start.13 = (pred[512,1024]{1,0:T(8,128)(4,1)}, pred[512,1024]{1,0:T(8,128)(4,1)S(1)}, u32[]{:S(2)}) copy-start(pred[512,1024]{1,0:T(8,128)(4,1)S(1)} %broadcast_compare_fusion.5) | copy-start | bytes 1572868 | tf_op jit(solution)/shard_map/while/body/eval_jaxpr/while
  1455.8 26.2 %copy-start.4 = (bf16[2,512,16,64]{1,3,2,0:T(8,128)(2,1)S(1)}, bf16[2,512,16,64]{1,3,2,0:T(8,128)(2,1)}, u32[]{:S(2)}) copy-start(bf16[2,512,16,64]{1,3,2,0:T(8,128)(2,1)} %get-tuple-element.648) | copy-start | bytes 6291460 | tf_op jit(solution)/shard_map/while/body/eval_jaxpr/while
  1536.6 18.9 %copy-start.23 = (f32[64,16,64]{0,2,1:T(8,128)S(1)}, f32[64,16,64]{0,2,1:T(8,128)}, u32[]{:S(2)}) copy-start(f32[64,16,64]{0,2,1:T(8,128)} %get-tuple-element.629) | copy-start | bytes 786436 | tf_op jit(solution)/shard_map/while/body/eval_jaxpr/while
  1580.1 112.0 %copy-start.1 = (bf16[1024,1024]{1,0:T(8,128)(2,1)S(1)}, bf16[1024,1024]{1,0:T(8,128)(2,1)}, u32[]{:S(2)}) copy-start(bf16[1024,1024]{1,0:T(8,128)(2,1)} %param.23) | copy-start | bytes 6291460
  1585.6 103.7 %copy-start.37 = (f32[2,64,1024]{2,1,0:T(8,128)S(1)}, f32[2,64,1024]{2,1,0:T(8,128)}, u32[]{:S(2)}) copy-start(f32[2,64,1024]{2,1,0:T(8,128)} %param.28) | copy-start | bytes 1572868
  1585.6 103.7 %copy-start.41 = (f32[2,64,1024]{2,1,0:T(8,128)S(1)}, f32[2,64,1024]{2,1,0:T(8,128)}, u32[]{:S(2)}) copy-start(f32[2,64,1024]{2,1,0:T(8,128)} %param.29) | copy-start | bytes 1572868
  (62 other events, 394.4 us)
Sparse Core Ops, SparseCore 0:
  156.6 230.2 all-gather.2
  454.9 280.8 reduce-scatter.2
  753.7 226.6 all-gather.4
  1012.5 280.8 reduce-scatter.4
  1562.4 126.9 all-reduce.1
where the time goes:
time: 1710 us; the launch traced here: 1700 us
  waiting for transfers between devices  1110 us (65%)
  matrix products  370 us (22%)
  other arithmetic  126 us (7%)
  local copies, waits for them, and re-layouts  73.3 us (4%)
    reduce_scatter x1, waiting for transfers between devices, on_device(): lax.psum_scatter(dot_right(grad_pre, w_in).astype(jnp.bfloat16), 'mp', sc...  280 us
    reduce_scatter x1, waiting for transfers between devices, on_device(): lax.psum_scatter(jnp.dot(activation, w_back, preferred_element_type=jnp.f...  277 us
    all_gather x1, waiting for transfers between devices, on_device(): lax.all_gather(normed_low, 'mp', axis=0, tiled=True)  230 us
    all_gather x1, waiting for transfers between devices, on_device(): lax.all_gather(grad_low, 'mp', axis=0, tiled=True)  227 us
    psum x1, waiting for transfers between devices, on_device(): prefix_grad = lax.psum(local_prefix, ('dp', 'mp'))  99.7 us
    dot_general x4, matrix products, block_scores(): jnp.einsum('bhd,khd->hbk', q_block, keys_row, preferred_element_type=jnp....  60.6 us
    convert_element_type x2, other arithmetic, one_block(): own_ds = (own_prob * (own_dot - center)).astype(jnp.bfloat16)  55.6 us
    dot_general x2, matrix products, one_block(): jnp.einsum('bhd,khd->hbk', g_block, values_row, preferred_element_type=jn...  51.5 us
  transfers between devices with their start and end apart: 5, of which 5 were waited for; matrix products, arithmetic and copies ran while one was open for 2% of the time, Pallas kernels for 0%

commit v1 on v0

v1 whole, which is shorter than its diff:
```python
import jax
import jax.numpy as jnp
from jax import lax
from jax.experimental import pallas as pl
from jax.experimental.pallas import tpu as pltpu
from jax.sharding import PartitionSpec as P

STEP = 5
HEAD_SCALE = 0.125

epsilon_norm = 1e-05
learn_rate = 1.0
weight_decay = 0.01
beta_one = 0.9
beta_two = 0.999
epsilon_adam = 1e-08

f32, bf16 = jnp.float32, jnp.bfloat16
NEG = -1e30
WIN = 256
KC = 64
QUAD = 256
NT = (((1,), (1,)), ((), ()))
NN = (((1,), (0,)), ((), ()))
TN = (((0,), (0,)), ((), ()))

def dot(a, b, d=NN):
    return lax.dot_general(a, b, d, preferred_element_type=f32)

def vm():
    return pl.BlockSpec(memory_space=pltpu.VMEM)

def sm():
    return pl.BlockSpec(memory_space=pltpu.SMEM)

def block_diag(piece):
    lane = lax.broadcasted_iota(jnp.int32, piece.shape, 1) // 64
    zero = jnp.zeros_like(piece)
    return jnp.concatenate([jnp.where(lane == h, piece, zero) for h in range(4)], axis=0)

def diag_of(full):
    lane = lax.broadcasted_iota(jnp.int32, (KC, 128), 1) < 64
    left = jnp.where(lane, full[0:64, 0:128], full[64:128, 0:128])
    right = jnp.where(lane, full[128:192, 128:256], full[192:256, 128:256])
    return jnp.concatenate([left, right], axis=1)

def window(lo_ref, seg_col_ref, seg_key_ref, c, w, length):
    nominal = lo_ref[c] + w * WIN
    start = pl.multiple_of(jnp.minimum(nominal, length - WIN), 16)
    rows = pl.ds(start, WIN)
    row_id = lax.broadcasted_iota(jnp.int32, (WIN, 128), 0) + start
    seg_q = seg_col_ref[rows, :]
    seg_k = seg_key_ref[pl.ds(c, 1), :]
    keep = jnp.logical_and(seg_q == seg_k, row_id >= nominal)
    bias = jnp.where(keep, 0.0, NEG)
    return rows, jnp.concatenate([bias, bias], axis=1)

def half_reduce(x, op, fill):
    lane = lax.broadcasted_iota(jnp.int32, x.shape, 1) < 64
    a = op(jnp.where(lane, x, fill), axis=1, keepdims=True)
    b = op(jnp.where(lane, fill, x), axis=1, keepdims=True)
    return jnp.where(lane, a, b)

def fwd_kernel(lo_ref, nw_ref, q_ref, k_ref, v_ref, pk_ref, pv_ref, segc_ref, segk_ref, att_ref, lse_ref, m_ref, l_ref, acc_ref, bdk_ref, bdv_ref):
    length, lanes = q_ref.shape
    quads = lanes // QUAD
    chunks = length // KC
    tiles = length // WIN
    for g in range(quads):
        cols = slice(g * QUAD, (g + 1) * QUAD)
        bdk_ref[g] = block_diag(pk_ref[:, cols])
        bdv_ref[g] = block_diag(pv_ref[:, cols])

    @pl.loop(0, tiles)
    def _(r):
        rows = pl.ds(pl.multiple_of(r * WIN, WIN), WIN)
        for g in range(quads):
            cols = slice(g * QUAD, (g + 1) * QUAD)
            m_ref[rows, cols] = dot(q_ref[rows, cols], bdk_ref[g], NT)

    def load_k(c, ref, bd):
        krows = pl.ds(pl.multiple_of(c * KC, KC), KC)
        for g in range(quads):
            bd[g] = block_diag(ref[krows, g * QUAD:(g + 1) * QUAD])

    @pl.loop(0, chunks)
    def _(c):
        load_k(c, k_ref, bdv_ref)

        @pl.loop(0, nw_ref[c])
        def _(w):
            rows, bias = window(lo_ref, segc_ref, segk_ref, c, w, length)
            parts = [slice(g * QUAD, (g + 1) * QUAD) for g in range(quads)]
            scores = [dot(q_ref[rows, cols], bdv_ref[g], NT) for g, cols in enumerate(parts)]
            for g, cols in enumerate(parts):
                m_ref[rows, cols] = jnp.maximum(m_ref[rows, cols], scores[g] + bias)

    for g in range(quads):
        bdv_ref[g] = block_diag(pv_ref[:, g * QUAD:(g + 1) * QUAD])

    @pl.loop(0, tiles)
    def _(r):
        rows = pl.ds(pl.multiple_of(r * WIN, WIN), WIN)
        for t in range(lanes // 128):
            cols = slice(t * 128, (t + 1) * 128)
            m_ref[rows, cols] = half_reduce(m_ref[rows, cols], jnp.max, NEG)
        parts = [slice(g * QUAD, (g + 1) * QUAD) for g in range(quads)]
        score = dot(q_ref[rows, parts[0]], bdk_ref[0], NT)
        for g, cols in enumerate(parts):
            later = dot(q_ref[rows, parts[g + 1]], bdk_ref[g + 1], NT) if g + 1 < quads else None
            p = jnp.exp(score - m_ref[rows, cols])
            l_ref[rows, cols] = p
            acc_ref[rows, cols] = dot(p.astype(bf16), bdv_ref[g])
            score = later

    @pl.loop(0, chunks)
    def _(c):
        load_k(c, k_ref, bdk_ref)
        load_k(c, v_ref, bdv_ref)

        @pl.loop(0, nw_ref[c])
        def _(w):
            rows, bias = window(lo_ref, segc_ref, segk_ref, c, w, length)
            parts = [slice(g * QUAD, (g + 1) * QUAD) for g in range(quads)]
            score = dot(q_ref[rows, parts[0]], bdk_ref[0], NT)
            for g, cols in enumerate(parts):
                later = dot(q_ref[rows, parts[g + 1]], bdk_ref[g + 1], NT) if g + 1 < quads else None
                p = jnp.exp(score + bias - m_ref[rows, cols])
                l_ref[rows, cols] += p
                acc_ref[rows, cols] += dot(p.astype(bf16), bdv_ref[g])
                score = later

    @pl.loop(0, tiles)
    def _(r):
        rows = pl.ds(pl.multiple_of(r * WIN, WIN), WIN)
        for t in range(lanes // 128):
            cols = slice(t * 128, (t + 1) * 128)
            total = half_reduce(l_ref[rows, cols], jnp.sum, 0.0)
            att_ref[rows, cols] = (acc_ref[rows, cols] / total).astype(bf16)
            lse_ref[rows, cols] = m_ref[rows, cols] + jnp.log(total)

def attend(lo, nw, q, k, v, pk, pv, segc, segk):
    length, lanes = q.shape
    quads = lanes // QUAD
    return pl.pallas_call(
        fwd_kernel,
        out_shape=(jax.ShapeDtypeStruct((length, lanes), bf16), jax.ShapeDtypeStruct((length, lanes), f32)),
        in_specs=[sm(), sm()] + [vm()] * 7,
        out_specs=(vm(), vm()),
        scratch_shapes=[pltpu.VMEM((length, lanes), f32)] * 3 + [pltpu.VMEM((quads, 256, 256), bf16)] * 2,
        compiler_params=pltpu.CompilerParams(vmem_limit_bytes=52 << 20),
        name="attend",
    )(lo, nw, q, k, v, pk, pv, segc, segk)

def windows(seg):
    length = seg.shape[0]
    chunks = length // KC
    by = seg.reshape(chunks, KC)
    first, last = by[:, 0], by[:, -1]
    lo = jnp.sum((seg[None, :] < first[:, None]).astype(jnp.int32), axis=1)
    hi = jnp.sum((seg[None, :] <= last[:, None]).astype(jnp.int32), axis=1)
    lo = lo // 16 * 16
    nw = (hi - lo + WIN - 1) // WIN
    segc = jnp.broadcast_to(seg[:, None], (length, 128))
    segk = jnp.concatenate([by, by], axis=1)
    return lo, nw, segc, segk

def pre_kernel(q_ref, g_ref, a_ref, lse_ref, pk_ref, pv_ref, delta_ref, ds_ref, dpk_ref, dpv_ref):
    length, lanes = q_ref.shape
    tiles = length // WIN
    bdk = block_diag(pk_ref[...])
    bdv = block_diag(pv_ref[...])
    row = lax.broadcasted_iota(jnp.int32, (QUAD, QUAD), 0) // 64
    lane = lax.broadcasted_iota(jnp.int32, (QUAD, QUAD), 1) // 64
    ones = jnp.where(row == lane, 1.0, 0.0).astype(bf16)
    dpk = jnp.zeros((KC, QUAD), f32)
    dpv = jnp.zeros((KC, QUAD), f32)
    spans = [slice(r * WIN, (r + 1) * WIN) for r in range(tiles)]

    def first(rows):
        g = g_ref[rows, :]
        prod = g.astype(f32) * a_ref[rows, :].astype(f32)
        high = prod.astype(bf16)
        rest = (prod - high.astype(f32)).astype(bf16)
        return dot(q_ref[rows, :], bdk, NT), dot(g, bdv, NT), dot(high, ones) + dot(rest, ones)

    def second(rows, three):
        delta_ref[rows, :] = three[2]
        p = jnp.exp(three[0] - lse_ref[rows, :])
        ds = (p * (three[1] - three[2])).astype(bf16)
        ds_ref[rows, :] = ds
        return p.astype(bf16), ds

    raw, done = first(spans[0]), None
    for r in range(tiles + 1):
        upcoming = first(spans[r + 1]) if r + 1 < tiles else None
        fresh = second(spans[r], raw) if r < tiles else None
        if done is not None:
            dpv = dpv + diag_of(dot(done[0], g_ref[spans[r - 1], :], TN))
            dpk = dpk + diag_of(dot(done[1], q_ref[spans[r - 1], :], TN))
        raw, done = upcoming, fresh
    dpk_ref[...] = dpk
    dpv_ref[...] = dpv

def prefix_back(q, g, a, lse, pk, pv):
    length, lanes = q.shape
    quads = lanes // QUAD
    slots = pk.shape[0]
    tall = pl.BlockSpec((length, QUAD), lambda i: (0, i))
    short = pl.BlockSpec((slots, QUAD), lambda i: (0, i))
    return pl.pallas_call(
        pre_kernel,
        grid=(quads,),
        out_shape=(jax.ShapeDtypeStruct((length, lanes), f32), jax.ShapeDtypeStruct((length, lanes), bf16),
                   jax.ShapeDtypeStruct((slots, lanes), f32), jax.ShapeDtypeStruct((slots, lanes), f32)),
        in_specs=[tall, tall, tall, tall, short, short],
        out_specs=(tall, tall, short, short),
        compiler_params=pltpu.CompilerParams(vmem_limit_bytes=48 << 20),
        name="prefix_back",
    )(q, g, a, lse, pk, pv)

def back_kernel(lo_ref, nw_ref, q_ref, k_ref, v_ref, g_ref, lse_ref, delta_ref, ds_ref, pk_ref, segc_ref, segk_ref,
                wq_ref, wk_ref, wv_ref, one_ref, out_ref, dq_ref, dk_ref, dv_ref, bdk_ref, bdv_ref, sk_ref, sv_ref):
    length, lanes = q_ref.shape
    quads = lanes // QUAD
    chunks = length // KC
    tiles = length // WIN
    for g in range(quads):
        cols = slice(g * QUAD, (g + 1) * QUAD)
        bdk_ref[g] = block_diag(pk_ref[:, cols])

    @pl.loop(0, tiles)
    def _(r):
        rows = pl.ds(pl.multiple_of(r * WIN, WIN), WIN)
        for g in range(quads):
            cols = slice(g * QUAD, (g + 1) * QUAD)
            dq_ref[rows, cols] = dot(ds_ref[rows, cols], bdk_ref[g])

    @pl.loop(0, chunks)
    def _(c):
        krows = pl.ds(pl.multiple_of(c * KC, KC), KC)
        for g in range(quads):
            cols = slice(g * QUAD, (g + 1) * QUAD)
            bdk_ref[g] = block_diag(k_ref[krows, cols])
            bdv_ref[g] = block_diag(v_ref[krows, cols])
        sk_ref[...] = jnp.zeros_like(sk_ref)
        sv_ref[...] = jnp.zeros_like(sv_ref)

        @pl.loop(0, nw_ref[c])
        def _(w):
            rows, bias = window(lo_ref, segc_ref, segk_ref, c, w, length)
            parts = [slice(g * QUAD, (g + 1) * QUAD) for g in range(quads)]

            def first(g):
                return dot(q_ref[rows, parts[g]], bdk_ref[g], NT), dot(g_ref[rows, parts[g]], bdv_ref[g], NT)

            def second(g, pair):
                p = jnp.exp(pair[0] + bias - lse_ref[rows, parts[g]])
                return p.astype(bf16), (p * (pair[1] - delta_ref[rows, parts[g]])).astype(bf16)

            def third(g, pair):
                cols = parts[g]
                sv_ref[:, cols] += diag_of(dot(pair[0], g_ref[rows, cols], TN))
                sk_ref[:, cols] += diag_of(dot(pair[1], q_ref[rows, cols], TN))
                dq_ref[rows, cols] += dot(pair[1], bdk_ref[g])

            raw, done = first(0), None
            for g in range(quads):
                upcoming = first(g + 1) if g + 1 < quads else None
                fresh = second(g, raw)
                if done is not None:
                    third(g - 1, done)
                raw, done = upcoming, fresh
            third(quads - 1, done)

        dk_ref[krows, :] = sk_ref[...].astype(bf16)
        dv_ref[krows, :] = sv_ref[...].astype(bf16)

    scale = HEAD_SCALE

    @pl.loop(0, tiles)
    def _(r):
        rows = pl.ds(pl.multiple_of(r * WIN, WIN), WIN)
        part = dot((dq_ref[rows, :] * scale).astype(bf16), wq_ref[...], NT)
        part = part + dot(dk_ref[rows, :], wk_ref[...], NT)
        part = part + dot(dv_ref[rows, :], wv_ref[...], NT)

        @pl.when(pl.program_id(0) == 0)
        def _():
            out_ref[rows, :] = one_ref[rows, :] + part

        @pl.when(pl.program_id(0) > 0)
        def _():
            out_ref[rows, :] += part

def attend_back(lo, nw, q, k, v, g, lse, delta, ds, pk, segc, segk, wq, wk, wv, grad_one, width=1024):
    length, lanes = q.shape
    quads = width // QUAD
    slots = pk.shape[0]
    tall = pl.BlockSpec((length, width), lambda i: (0, i))
    short = pl.BlockSpec((slots, width), lambda i: (0, i))
    wt = pl.BlockSpec((lanes, width), lambda i: (0, i))

    def whole(shape):
        return pl.BlockSpec(shape, lambda i: (0, 0))

    smem = pl.BlockSpec(memory_space=pltpu.SMEM)
    return pl.pallas_call(
        back_kernel,
        grid=(lanes // width,),
        out_shape=jax.ShapeDtypeStruct((length, lanes), f32),
        in_specs=[smem, smem, tall, tall, tall, tall, tall, tall, tall, short, whole(segc.shape), whole(segk.shape), wt, wt, wt, whole(grad_one.shape)],
        out_specs=whole((length, lanes)),
        scratch_shapes=[pltpu.VMEM((length, width), f32), pltpu.VMEM((length, width), bf16), pltpu.VMEM((length, width), bf16),
                        pltpu.VMEM((quads, 256, 256), bf16), pltpu.VMEM((quads, 256, 256), bf16),
                        pltpu.VMEM((KC, width), f32), pltpu.VMEM((KC, width), f32)],
        compiler_params=pltpu.CompilerParams(vmem_limit_bytes=58 << 20),
        name="attend_back",
    )(lo, nw, q, k, v, g, lse, delta, ds, pk, segc, segk, wq, wk, wv, grad_one)


def mean_of(x):
    return jnp.mean(x, axis=-1, keepdims=True)


def norm_kernel(att_ref, tok_ref, wout_ref, gain_ref, hat_ref, inv_ref, low_ref):
    x = tok_ref[...].astype(f32) + dot(att_ref[...], wout_ref[...])
    centred = x - mean_of(x)
    inv = lax.rsqrt(mean_of(centred * centred) + epsilon_norm)
    hat = centred * inv
    hat_ref[...] = hat
    inv_ref[...] = jnp.broadcast_to(inv, inv_ref.shape)
    low_ref[...] = (gain_ref[...] * hat).astype(bf16)


def first_norm(att, tokens, w_out, gain):
    length, lanes = att.shape
    tall = pl.BlockSpec((WIN, lanes), lambda i: (i, 0))
    return pl.pallas_call(
        norm_kernel,
        grid=(length // WIN,),
        out_shape=(
            jax.ShapeDtypeStruct((length, lanes), f32),
            jax.ShapeDtypeStruct((length, 128), f32),
            jax.ShapeDtypeStruct((length, lanes), bf16),
        ),
        in_specs=[
            tall,
            tall,
            pl.BlockSpec((lanes, lanes), lambda i: (0, 0)),
            pl.BlockSpec((1, lanes), lambda i: (0, 0)),
        ],
        out_specs=(tall, pl.BlockSpec((WIN, 128), lambda i: (i, 0)), tall),
        compiler_params=pltpu.CompilerParams(vmem_limit_bytes=40 << 20),
        name="first_norm",
    )(att, tokens, w_out, gain)


def gelu_pair(x):
    t = 1.0 / (1.0 + (0.3275911 * 0.7071067811865476) * jnp.abs(x))
    bell = jnp.exp(-0.5 * (x * x))
    poly = t * (0.127414796 + t * (-0.142248368 + t * (0.7107068705 + t * (-0.7265760135 + t * 0.5307027145))))
    tail = poly * bell
    phi = jnp.where(x < 0.0, tail, 1.0 - tail)
    return x * phi, phi + x * (0.3989422804014327 * bell)


HID = 512


def ffn_kernel(low_ref, w_in_ref, w_back_ref, start_ref, sum_ref, slope_ref):
    length = low_ref.shape[0]
    tiles = length // WIN
    spans = [slice(r * WIN, (r + 1) * WIN) for r in range(tiles)]

    @pl.when(pl.program_id(0) == 0)
    def _():
        sum_ref[...] = start_ref[...]

    def first(r):
        return dot(low_ref[spans[r], :], w_in_ref[...], NT)

    def second(r, x):
        act, slope = gelu_pair(x)
        slope_ref[spans[r], :] = slope.astype(bf16)
        return act.astype(bf16)

    raw, done = first(0), None
    for r in range(tiles + 1):
        upcoming = first(r + 1) if r + 1 < tiles else None
        fresh = second(r, raw) if r < tiles else None
        if done is not None:
            sum_ref[spans[r - 1], :] += dot(done, w_back_ref[...])
        raw, done = upcoming, fresh


def ffn_forward(low, w_in, w_back, start):
    length, lanes = low.shape
    hidden = w_in.shape[0]

    def whole(shape):
        return pl.BlockSpec(shape, lambda i: (0, 0))

    wt = pl.BlockSpec((HID, lanes), lambda i: (i, 0))
    return pl.pallas_call(
        ffn_kernel,
        grid=(hidden // HID,),
        out_shape=(jax.ShapeDtypeStruct((length, lanes), f32), jax.ShapeDtypeStruct((length, hidden), bf16)),
        in_specs=[whole(low.shape), wt, wt, whole(start.shape)],
        out_specs=(whole((length, lanes)), pl.BlockSpec((length, HID), lambda i: (0, i))),
        compiler_params=pltpu.CompilerParams(vmem_limit_bytes=48 << 20),
        name="ffn_forward",
    )(low, w_in, w_back, start)


def ffn_back_kernel(
    sum_ref, cot_ref, gain_two_ref, gain_one_ref, w_in_ref, w_back_ref, slope_ref, hat_ref, inv_ref, w_out_ref,
    layer_ref, one_ref, att_ref, acc_ref, low_ref,
):
    length = sum_ref.shape[0]
    tiles = length // WIN
    spans = [slice(r * WIN, (r + 1) * WIN) for r in range(tiles)]

    @pl.when(pl.program_id(0) == 0)
    def _():
        for rows in spans:
            x = sum_ref[rows, :]
            centred = x - mean_of(x)
            inv = lax.rsqrt(mean_of(centred * centred) + epsilon_norm)
            hat = centred * inv
            layer_ref[rows, :] = (gain_two_ref[...] * hat).astype(bf16)
            pull = cot_ref[rows, :].astype(f32) * gain_two_ref[...]
            grad = inv * (pull - mean_of(pull) - hat * mean_of(pull * hat))
            acc_ref[rows, :] = grad
            low_ref[rows, :] = grad.astype(bf16)

    def first(r):
        return dot(low_ref[spans[r], :], w_back_ref[...], NT)

    def second(r, x):
        return (x * slope_ref[spans[r], :].astype(f32)).astype(bf16)

    raw, done = first(0), None
    for r in range(tiles + 1):
        upcoming = first(r + 1) if r + 1 < tiles else None
        fresh = second(r, raw) if r < tiles else None
        if done is not None:
            acc_ref[spans[r - 1], :] += dot(done, w_in_ref[...])
        raw, done = upcoming, fresh

    @pl.when(pl.program_id(0) == pl.num_programs(0) - 1)
    def _():
        for rows in spans:
            pull = acc_ref[rows, :] * gain_one_ref[...]
            hat = hat_ref[rows, :]
            grad = inv_ref[rows, 0:1] * (pull - mean_of(pull) - hat * mean_of(pull * hat))
            one_ref[rows, :] = grad
            att_ref[rows, :] = dot(grad.astype(bf16), w_out_ref[...], NT).astype(bf16)


def ffn_backward(total, cot, gain_two, gain_one, w_in, w_back, slope, hat, inv, w_out):
    length, lanes = total.shape
    hidden = w_in.shape[0]

    def whole(array):
        return pl.BlockSpec(array.shape, lambda i: (0, 0))

    wt = pl.BlockSpec((HID, lanes), lambda i: (i, 0))
    outs = (
        jax.ShapeDtypeStruct((length, lanes), bf16),
        jax.ShapeDtypeStruct((length, lanes), f32),
        jax.ShapeDtypeStruct((length, lanes), bf16),
    )
    return pl.pallas_call(
        ffn_back_kernel,
        grid=(hidden // HID,),
        out_shape=outs,
        in_specs=[
            whole(total), whole(cot), whole(gain_two), whole(gain_one), wt, wt,
            pl.BlockSpec((length, HID), lambda i: (0, i)), whole(hat), whole(inv), whole(w_out),
        ],
        out_specs=tuple(whole(o) for o in outs),
        scratch_shapes=[pltpu.VMEM((length, lanes), f32), pltpu.VMEM((length, lanes), bf16)],
        compiler_params=pltpu.CompilerParams(vmem_limit_bytes=60 << 20),
        name="ffn_backward",
    )(total, cot, gain_two, gain_one, w_in, w_back, slope, hat, inv, w_out)


def gather_weights(w_in, w_back):
    copies = lax.axis_size("dp")
    part = w_in.shape[1] // copies
    place = lax.axis_index("dp") * part
    mine_in = lax.dynamic_slice_in_dim(w_in, place, part, 1).T
    mine_back = lax.dynamic_slice_in_dim(w_back, place, part, 0)
    return (
        lax.all_gather(mine_in, ("dp", "mp"), axis=0, tiled=True),
        lax.all_gather(mine_back, ("dp", "mp"), axis=0, tiled=True),
    )


def on_device(
    tokens, segment_ids, w_query, w_key, w_value, w_out, gain_one, gain_two, w_in, w_back,
    prefix_master, moment_one, moment_two, cotangent,
):
    all_in, all_back = gather_weights(w_in, w_back)
    prefix_low = prefix_master.astype(bf16)
    prefix_keys, prefix_vals = prefix_low[0], prefix_low[1]
    first_gain, second_gain = gain_one[None, :], gain_two[None, :]

    queries = (jnp.dot(tokens, w_query, preferred_element_type=f32) * HEAD_SCALE).astype(bf16)
    keys_own = jnp.dot(tokens, w_key, preferred_element_type=f32).astype(bf16)
    values_own = jnp.dot(tokens, w_value, preferred_element_type=f32).astype(bf16)
    lo, nw, segc, segk = windows(segment_ids[0])
    attended, lse = attend(lo, nw, queries, keys_own, values_own, prefix_keys, prefix_vals, segc, segk)
    hat, inv, normed_low = first_norm(attended, tokens, w_out, first_gain)
    total, slope = ffn_forward(normed_low, all_in, all_back, first_gain * hat)
    layer_output, grad_one, grad_att = ffn_backward(
        total, cotangent, second_gain, first_gain, all_in, all_back, slope, hat, inv, w_out
    )
    delta, ds_prefix, dpk, dpv = prefix_back(queries, grad_att, attended, lse, prefix_keys, prefix_vals)
    prefix_grad = lax.psum(jnp.stack([dpk, dpv]), ("dp", "mp"))
    input_grad = attend_back(
        lo, nw, queries, keys_own, values_own, grad_att, lse, delta, ds_prefix, prefix_keys, segc, segk,
        w_query, w_key, w_value, grad_one,
    )
    new_first = beta_one * moment_one + (1.0 - beta_one) * prefix_grad
    new_second = beta_two * moment_two + (1.0 - beta_two) * prefix_grad * prefix_grad
    first_hat = new_first / (1.0 - beta_one**STEP)
    second_hat = new_second / (1.0 - beta_two**STEP)
    new_master = prefix_master * (1.0 - learn_rate * weight_decay) - learn_rate * first_hat / (
        jnp.sqrt(second_hat) + epsilon_adam
    )
    return (layer_output, input_grad, new_master, new_first, new_second, new_master.astype(bf16))


def solution(mesh):
    rows = P(("dp", "mp"), None)
    return jax.shard_map(
        on_device,
        mesh=mesh,
        in_specs=(rows, rows, P(), P(), P(), P(), P(), P(), P(None, "mp"), P("mp", None), P(), P(), P(), rows),
        out_specs=(rows, rows, P(), P(), P(), P()),
        check_vma=False,
    )
```

time: 1710 us -> 384 us (0.22)
  waiting for transfers between devices: 1110 us -> 174 us
  matrix products: 370 us -> 12.8 us
  Pallas kernels: 0 us -> 163 us
  other arithmetic: 126 us -> 8.27 us
  local copies, waits for them, and re-layouts: 73.3 us -> 11.8 us
    reduce_scatter x2 -> x0, waiting for transfers between devices: 557 us -> none  [the longest x1 280 us: on_device(): lax.psum_scatter(dot_right(grad_pre, w_in).astype(jnp.bfloat16), 'mp', sc...]
    all_gather x2, waiting for transfers between devices: 457 us -> 94.4 us  [the longest x1 79.6 us: gather_weights(): lax.all_gather(mine_back, ('dp', 'mp'), axis=0, tiled=True)]
    dot_general x39 -> x3, matrix products: 370 us -> 12.8 us  [the longest x1 5.44 us: on_device(): jnp.dot(tokens, w_query, preferred_element_type=f32) * HEAD_SCALE]
    pallas_call x0 -> x6, Pallas kernels: none -> 163 us  [the longest x1 47.3 us: attend_back(): pl.pallas_call(back_kernel, grid=(lanes // width,), out_shape=jax.ShapeDt...]
    convert_element_type x10 -> x2, other arithmetic: 70.5 us -> 3.6 us  [the longest x1 2.53 us: on_device(): new_master.astype(bf16)]
    reduce_sum x10 -> x1, other arithmetic: 52.4 us -> 0.2 us  [windows(): hi = jnp.sum((seg[None, :] <= last[:, None]).astype(jnp.int32), axis=1)]
    unnamed x99 -> x48, local copies, waits for them, and re-layouts: 35 us -> 9.59 us
    psum x1, waiting for transfers between devices: 99.7 us -> 79.3 us  [on_device(): prefix_grad = lax.psum(jnp.stack([dpk, dpv]), ('dp', 'mp'))]
  transfers between devices with their start and end apart: 5 -> 3, of which waited for: 5 -> 3; matrix products, arithmetic and copies ran while one was open for 2% -> 5% of each run, Pallas kernels for 0% -> 23%
where the time goes in v1:
time: 384 us; the launch traced here: 383 us
  waiting for transfers between devices  174 us (45%)
  Pallas kernels  163 us (42%)
  between operations  14 us (4%)
  matrix products  12.8 us (3%)
  local copies, waits for them, and re-layouts  11.8 us (3%)
  other arithmetic  8.27 us (2%)
    all_gather x1, waiting for transfers between devices, gather_weights(): lax.all_gather(mine_back, ('dp', 'mp'), axis=0, tiled=True)  79.6 us
    psum x1, waiting for transfers between devices, on_device(): prefix_grad = lax.psum(jnp.stack([dpk, dpv]), ('dp', 'mp'))  79.3 us
    pallas_call x1, Pallas kernels, attend_back(): pl.pallas_call(back_kernel, grid=(lanes // width,), out_shape=jax.ShapeDt...  47.3 us
    pallas_call x1, Pallas kernels, attend(): pl.pallas_call(fwd_kernel, out_shape=(jax.ShapeDtypeStruct((length, lanes...  37.1 us
    pallas_call x1, Pallas kernels, ffn_backward(): pl.pallas_call(ffn_back_kernel, grid=(hidden // HID,), out_shape=outs, in...  35.1 us
    pallas_call x1, Pallas kernels, ffn_forward(): pl.pallas_call(ffn_kernel, grid=(hidden // HID,), out_shape=(jax.ShapeDty...  31.3 us
    all_gather x1, waiting for transfers between devices, gather_weights(): lax.all_gather(mine_in, ('dp', 'mp'), axis=0, tiled=True)  14.8 us
    unnamed x48, local copies, waits for them, and re-layouts  9.59 us
  transfers between devices with their start and end apart: 3, of which 3 were waited for; matrix products, arithmetic and copies ran while one was open for 5% of the time, Pallas kernels for 23%

profile of v1, /device:TPU:0, one launch (start us, length us, event | category | flops | bytes accessed | tf_op | source)
XLA Modules:
  0.0 383.3 jit_solution(17086046737831177585)
XLA Ops:
  7.3 1.1 copy-done
  8.4 0.9 copy.23
  9.4 1.7 constant_dynamic-slice_fusion
  12.4 1.1 convert_element_type.26
  14.0 5.4 %multiply_convert_fusion.q_ref = bf16[1024,1024]{1,0:T(8,128)(2,1)} fusion(bf16[1024,1024]{1,0:T(8,128)(2,1)S(1)} %copy-done.9, bf16[1024,1024]{1,0:T(8,128)(2,1)} %wq_ref.1), kind=kOutput, calls=%fused_computation | convolution fusion | flops 2149580800 | bytes 6291456 | tf_op jit(solution)/shard_map/dot_general | solution.py:510
  19.5 3.7 convolution_convert_fusion.1.k_ref
  23.1 3.7 convolution_convert_fusion.v_ref
  27.1 37.1 %attend.1 = (bf16[1024,1024]{1,0:T(8,128)(2,1)}, f32[1024,1024]{1,0:T(8,128)}) custom-call(s32[16]{0:T(128)S(1)} %get-tuple-element.43.lo_ref, s32[16]{0:T(128)S(1)} %get-tuple-element.42.nw_ref, bf16[1024,1024]{1,0:T(8,128)(2,1)} %multiply_convert_fusion.q_ref, bf16[1024,1024]{1,0:T(8,128)(2,1)} %convolution_convert_fusion.1.k_ref, ...), custom_call_target="tpu_custom_call" | custom-call | tf_op jit(solution)/shard_map/attend/pallas_call | solution.py:145
  64.2 1.6 copy-done.4
  65.8 4.0 %first_norm.1 = (f32[1024,1024]{1,0:T(8,128)S(1)}, f32[1024,128]{1,0:T(8,128)S(1)}, bf16[1024,1024]{1,0:T(8,128)(2,1)S(1)}) custom-call(bf16[1024,1024]{1,0:T(8,128)(2,1)S(1)} %copy-done.4, bf16[1024,1024]{1,0:T(8,128)(2,1)S(1)} %copy-done.9, bf16[1024,1024]{1,0:T(8,128)(2,1)S(1)} %copy-done.5, f32[1,1024]{1,0:T(1,128)S(1)} %bitcast.19), custom_call_target="tpu_custom_call" | custom-call | tf_op jit(solution)/shard_map/first_norm/pallas_call | solution.py:339
  69.8 1.3 copy-done.10
  71.1 0.8 copy-done.12
  71.9 2.0 copy-done.3
  73.9 2.9 broadcast_multiply_fusion.start_ref
  76.8 14.8 %all-gather.3.cloned.1.call-done.w_in_ref = bf16[4096,1024]{1,0:T(8,128)(2,1)} async-done(((bf16[128,1024]{1,0:T(8,128)(2,1)}), bf16[4096,1024]{1,0:T(8,128)(2,1)}) %all-gather.3.cloned.1.call-update) | async-done | bytes 8388624 | tf_op jit(solution)/shard_map/all_gather | solution.py:496
  91.6 79.6 %all-gather.5.cloned.1.call-done.w_back_ref = bf16[4096,1024]{1,0:T(8,128)(2,1)} async-done(((bf16[128,1024]{1,0:T(8,128)(2,1)}), bf16[4096,1024]{1,0:T(8,128)(2,1)}) %all-gather.5.cloned.1.call-update) | async-done | bytes 8388624 | tf_op jit(solution)/shard_map/all_gather | solution.py:497
  171.2 31.3 %ffn_forward.1 = (f32[1024,1024]{1,0:T(8,128)}, bf16[1024,4096]{1,0:T(8,128)(2,1)}) custom-call(bf16[1024,1024]{1,0:T(8,128)(2,1)S(1)} %copy-done.11, bf16[4096,1024]{1,0:T(8,128)(2,1)} %all-gather.3.cloned.1.call-done.w_in_ref, bf16[4096,1024]{1,0:T(8,128)(2,1)} %all-gather.5.cloned.1.call-done.w_back_ref, f32[1024,1024]{1,0:T(8,128)} %broadcast_multiply_fusion.start_ref), custom_call_target="tpu_custom_call" | custom-call | tf_op jit(solution)/shard_map/ffn_forward/pallas_call | solution.py:405
  202.5 35.1 %ffn_backward.1 = (bf16[1024,1024]{1,0:T(8,128)(2,1)}, f32[1024,1024]{1,0:T(8,128)}, bf16[1024,1024]{1,0:T(8,128)(2,1)}) custom-call(f32[1024,1024]{1,0:T(8,128)} %get-tuple-element.23.sum_ref, bf16[1024,1024]{1,0:T(8,128)(2,1)} %cot_ref.1, f32[1,1024]{1,0:T(1,128)} %bitcast.23, f32[1,1024]{1,0:T(1,128)} %bitcast.18, ...), custom_call_target="tpu_custom_call" | custom-call | tf_op jit(solution)/shard_map/ffn_backward/pallas_call | solution.py:474
  237.6 7.9 %prefix_back.1 = (f32[1024,1024]{1,0:T(8,128)}, bf16[1024,1024]{1,0:T(8,128)(2,1)S(1)}, f32[64,1024]{1,0:T(8,128)S(1)}, f32[64,1024]{1,0:T(8,128)S(1)}) custom-call(bf16[1024,1024]{1,0:T(8,128)(2,1)S(1)} %copy-done.2, bf16[1024,1024]{1,0:T(8,128)(2,1)} %get-tuple-element.27.g_ref, bf16[1024,1024]{1,0:T(8,128)(2,1)} %get-tuple-element.20.att_ref.a_ref, ...), custom_call_target="tpu_custom_call" | custom-call | tf_op jit(solution)/shard_map/prefix_back/pallas_call | solution.py:211
  245.4 1.3 copy-done.8
  246.7 0.8 pad_maximum_fusion
  247.7 47.3 %attend_back.1 = f32[1024,1024]{1,0:T(8,128)} custom-call(s32[16]{0:T(128)} %copy-done.16, s32[16]{0:T(128)} %copy-done.15, bf16[1024,1024]{1,0:T(8,128)(2,1)} %multiply_convert_fusion.q_ref, bf16[1024,1024]{1,0:T(8,128)(2,1)} %convolution_convert_fusion.1.k_ref, bf16[1024,1024]{1,0:T(8,128)(2,1)} %convolution_convert_fusion.v_ref, ...), custom_call_target="tpu_custom_call" | custom-call | tf_op jit(solution)/shard_map/attend_back/pallas_call | solution.py:308
  294.9 79.3 %all-reduce.2.cloned.1.call-done = f32[2,64,1024]{2,1,0:T(8,128)} async-done(((f32[2,64,1024]{2,1,0:T(8,128)}), f32[2,64,1024]{2,1,0:T(8,128)}) %all-reduce.2.cloned.1.call-update) | async-done | bytes 524304 | tf_op jit(solution)/shard_map/psum | solution.py:521
  374.2 2.5 fusion.2
  (56 shorter events, 2.2 us)
Async XLA Ops:
  7.2 4.4 %copy-start.22 = (s32[1,1024]{1,0:T(1,128)S(1)}, s32[1,1024]{1,0:T(1,128)}, u32[]{:S(2)}) copy-start(s32[1,1024]{1,0:T(1,128)} %param.15) | copy-start | bytes 12292
  7.2 6.8 %copy-start.9 = (bf16[1024,1024]{1,0:T(8,128)(2,1)S(1)}, bf16[1024,1024]{1,0:T(8,128)(2,1)}, u32[]{:S(2)}) copy-start(bf16[1024,1024]{1,0:T(8,128)(2,1)} %tok_ref.1) | copy-start | bytes 6291460
  7.2 84.4 %all-gather.3.cloned.1.call-start = ((), (), s32[]{:S(2)}) async-start(), calls=%async_computation | async-start | bytes 8650752 | tf_op jit(solution)/shard_map/all_gather | solution.py:496
  9.3 161.9 %all-gather.5.cloned.1.call-start = ((), (), s32[]{:S(2)}) async-start(), calls=%async_computation.1 | async-start | bytes 8650752 | tf_op jit(solution)/shard_map/all_gather | solution.py:497
  11.1 363.1 %all-reduce.2.cloned.1.call-start = ((), (), s32[]{:S(2)}) async-start(), calls=%async_computation.2 | async-start | bytes 1048576 | tf_op jit(solution)/shard_map/psum | solution.py:521
  13.5 13.5 %copy-start.13 = (s32[16,128]{1,0:T(8,128)}, s32[16,128]{1,0:T(8,128)S(1)}, u32[]{:S(2)}) copy-start(s32[16,128]{1,0:T(8,128)S(1)} %pad_add_fusion.segk_ref) | copy-start | bytes 24580
  13.9 13.1 %copy-start.15 = (s32[16]{0:T(128)}, s32[16]{0:T(128)S(1)}, u32[]{:S(2)}) copy-start(s32[16]{0:T(128)S(1)} %get-tuple-element.42.nw_ref) | copy-start | bytes 196
  13.9 13.1 %copy-start.16 = (s32[16]{0:T(128)}, s32[16]{0:T(128)S(1)}, u32[]{:S(2)}) copy-start(s32[16]{0:T(128)S(1)} %get-tuple-element.43.lo_ref) | copy-start | bytes 196
  14.0 223.6 %copy-start.7 = (bf16[64,1024]{1,0:T(8,128)(2,1)}, bf16[64,1024]{1,0:T(8,128)(2,1)S(1)}, u32[]{:S(2)}) copy-start(bf16[64,1024]{1,0:T(8,128)(2,1)S(1)} %get-tuple-element.45.pk_ref) | copy-start | bytes 393220
  14.0 5.5 %copy-start.17 = (bf16[1024,1024]{1,0:T(8,128)(2,1)S(1)}, bf16[1024,1024]{1,0:T(8,128)(2,1)}, u32[]{:S(2)}) copy-start(bf16[1024,1024]{1,0:T(8,128)(2,1)} %wk_ref.1) | copy-start | bytes 6291460
  19.5 3.7 copy-start.18
  27.0 37.2 %copy-start.6 = (s32[1024,128]{1,0:T(8,128)}, s32[1024,128]{1,0:T(8,128)S(1)}, u32[]{:S(2)}) copy-start(s32[1024,128]{1,0:T(8,128)S(1)} %broadcast_in_dim.11.segc_ref) | copy-start | bytes 1572868
  27.0 37.2 %copy-start.5 = (bf16[1024,1024]{1,0:T(8,128)(2,1)S(1)}, bf16[1024,1024]{1,0:T(8,128)(2,1)}, u32[]{:S(2)}) copy-start(bf16[1024,1024]{1,0:T(8,128)(2,1)} %w_out_ref.1) | copy-start | bytes 6291460
  27.1 37.1 %copy-start.14 = (f32[1024]{0:T(1024)S(1)}, f32[1024]{0:T(1024)}, u32[]{:S(2)}) copy-start(f32[1024]{0:T(1024)} %param.20) | copy-start | bytes 12292
  64.2 1.6 copy-start.4
  69.8 1.3 copy-start.10
  71.9 2.0 copy-start.3
  73.9 97.3 %copy-start.11 = (bf16[1024,1024]{1,0:T(8,128)(2,1)S(1)}, bf16[1024,1024]{1,0:T(8,128)(2,1)}, u32[]{:S(2)}) copy-start(bf16[1024,1024]{1,0:T(8,128)(2,1)} %copy-done.10) | copy-start | bytes 6291460
  202.5 35.1 %copy-start.2 = (bf16[1024,1024]{1,0:T(8,128)(2,1)S(1)}, bf16[1024,1024]{1,0:T(8,128)(2,1)}, u32[]{:S(2)}) copy-start(bf16[1024,1024]{1,0:T(8,128)(2,1)} %multiply_convert_fusion.q_ref) | copy-start | bytes 6291460
  245.4 1.3 copy-start.8
  247.6 126.6 %copy-start.19 = (f32[2,64,1024]{2,1,0:T(8,128)S(1)}, f32[2,64,1024]{2,1,0:T(8,128)}, u32[]{:S(2)}) copy-start(f32[2,64,1024]{2,1,0:T(8,128)} %param.24) | copy-start | bytes 1572868
  247.6 126.6 %copy-start.20 = (f32[2,64,1024]{2,1,0:T(8,128)S(1)}, f32[2,64,1024]{2,1,0:T(8,128)}, u32[]{:S(2)}) copy-start(f32[2,64,1024]{2,1,0:T(8,128)} %param.25) | copy-start | bytes 1572868
  247.6 126.6 %copy-start.21 = (f32[2,64,1024]{2,1,0:T(8,128)S(1)}, f32[2,64,1024]{2,1,0:T(8,128)}, u32[]{:S(2)}) copy-start(f32[2,64,1024]{2,1,0:T(8,128)} %param.26) | copy-start | bytes 1572868
  247.7 129.1 %copy-start.1 = (bf16[1024,512]{1,0:T(8,128)(2,1)S(1)}, bf16[1024,512]{1,0:T(8,128)(2,1)}, u32[]{:S(2)}) copy-start(bf16[1024,512]{1,0:T(8,128)(2,1)} %param.22) | copy-start | bytes 3145732
  (2 other events, 2.0 us)
Sparse Core Ops, SparseCore 0:
  11.6 79.9 all-gather.2
  95.2 75.9 all-gather.4
  247.7 126.4 all-reduce.1
